TPU v7x, 256 devices: a whole 4x4x8 slice. The times are simulated.
256 devices in a mesh: seq: 2 (over core), tp: 4 (over x), req: 32 (over z, y).
Axes of the slice: x: 4, y: 4, z: 8, core: 2. Of those that a mesh axis runs over, the one named last changes fastest.
Arguments:
- cache_pool: bfloat16 [2, 32, 8, 16, 128, 256], P('seq', 'req', 'tp'), may hold values from -6 to 6
- fresh_kv: bfloat16 [32, 8, 256, 256], P('req', 'tp', 'seq'), may hold values from -6.2 to 6.2
- queries: bfloat16 [32, 256, 12288], P('req', 'seq', 'tp'), may hold values from -155 to 155
- stretch_owner: int32 [32, 2], replicated, may hold values from 0 to 48, as said below
- stretch_slot: int32 [32, 2], replicated, may hold values from 0 to 15
- recomp: int32 [32, 2, 1], replicated, may hold values from -1 to 15, as said below
Outputs:
- attended: bfloat16 [32, 256, 12288], P('req', 'seq', 'tp')
- deviation: float32 [32, 256], P('req', 'seq')
Inputs may be any that keep to these rules, and one draw needn't show every extreme that they name: `stretch_owner`: every entry is a multiple of 16; the passage's tile t lies on owner stretch_owner + t, counting owners seq-major over seq and req. `recomp`: the entries of one passage's list that are not -1 differ from each other.
All inputs are finite; a program needn't handle non-finite values.
Results may differ from a plain program's by a relative error of at most 0.0049.
Values may be sent and summed in bfloat16 or wider, within the bound.
A program may use at most 64 MiB of HBM per device.

v0:
```python
import functools

import jax
import jax.numpy as jnp
from jax import lax
from jax.experimental import pallas as pl
from jax.experimental.pallas import tpu as pltpu
from jax.sharding import PartitionSpec as P

KVH = 8
HD = 128
TILE = 128
NT = 16
PER_KV = 12
HCOLS = PER_KV * HD
NZ = 8
NY = 4
MESH = pl.DeviceIdType.MESH
SCALE = HD**-0.5 * 1.4426950408889634
LOW = -1e30
LEVELS = ((11, 9, 6, 3), (13, 10, 7, 3), (15, 12, 9, 4), (28, 20, 12, 4))


def bits_set(word):
    shift = lax.shift_right_logical
    word = word - (shift(word, 1) & 0x55555555)
    word = (word & 0x33333333) + (shift(word, 2) & 0x33333333)
    word = (word + shift(word, 4)) & 0x0F0F0F0F
    word = word + shift(word, 8)
    return (word + shift(word, 16)) & 63


def prepare_kernel(owner, slot, recomp, tab, level, whole, column):
    me = lax.axis_index("req")
    z, y = me // NY, lax.rem(me, NY)

    def passage(r, c):
        block = owner[c, r] // NT
        side = lax.rem(block, 2)
        first, second = recomp[0, r], recomp[1, r]
        second = jnp.maximum(second + 1, 0)
        reach = second if c else jnp.where(second > 0, NT, jnp.maximum(first + 1, 0))
        return reach, side, (block // 2) * NT + slot[c, r]

    def read(row, carry):
        sets = {}
        for q in range(2 * NY):
            reach, side, e = passage(row * NY + q // 2, q % 2)
            bit = jnp.left_shift(1, e)
            low = jnp.where(side == 0, bit, 0)
            for group in range(4):
                for which, tile in ((0, NY * group), (1, NY * group + y)):
                    for k, part in ((group, low), (group + 4, bit ^ low)):
                        key = (which, k, (q // 2) % 2)
                        part = jnp.where(reach > tile, part, 0)
                        sets[key] = sets[key] | part if key in sets else part
        for (which, k, odd), word in sets.items():
            (whole, column)[which][(k * NZ + row) * 2 + odd] = word
        return carry

    lax.fori_loop(0, NZ, read, 0)

    def needs(ref, k, d, way):
        at = (k * NZ + lax.rem(k + (d if way == 0 else -d) + NZ, NZ)) * 2
        return ref[at + way] if d == 4 else ref[at] | ref[at + 1]

    def count(k, most):
        most = list(most)
        for way in range(2):
            seen = jnp.int32(0)
            for d in (4, 3, 2, 1):
                seen = seen | needs(whole, k, d, way)
                most[d - 1] = jnp.maximum(most[d - 1], bits_set(seen))
        return tuple(most)

    most = lax.fori_loop(0, NZ, count, (jnp.int32(0),) * 4)
    pick = jnp.int32(0)
    for caps in LEVELS[:-1]:
        over = functools.reduce(jnp.logical_or, [m > cap for m, cap in zip(most, caps)])
        pick = pick + jnp.where(over, 1, 0)
    level[0] = pick

    def walk(k, way, far):
        seen, groups = jnp.int32(0), []
        for d in range(4, far - 1, -1):
            wanted = needs(column, k, d, way)
            groups.append((wanted & ~seen, bits_set(seen)))
            seen = seen | wanted
        return groups

    def locate(e, groups):
        bit = jnp.left_shift(1, e)
        word, base = jnp.int32(0), jnp.int32(0)
        for new, start in groups:
            has = (new & bit) != 0
            word, base = jnp.where(has, new, word), jnp.where(has, start, base)
        return jnp.where(word != 0, base + bits_set(word & (bit - 1)), 0), word != 0

    for i in range(64):
        tab[i] = 0
    for way, sign in ((0, 1), (1, -1)):
        groups = walk(z, way, 1)
        for d, group in zip((4, 3, 2, 1), groups):
            row = lax.rem(z + sign * d + NZ, NZ)

            def send(q, carry):
                c = lax.rem(q, 2)
                r = row * NY + q // 2
                e = (owner[c, r] // (2 * NT)) * NT + slot[c, r]
                place, found = locate(e, [group])
                tab[jnp.where(found, way * 32 + place, 130)] = e
                return carry

            lax.fori_loop(0, 2 * NY, send, 0, unroll=True)
    for c in range(2):
        tab[128 + c] = recomp[c, me]
    here = [passage(me - y + q // 2, q % 2) for q in range(2 * NY)]
    for j in range(4):
        lists = []
        for way, sign in ((0, 1), (1, -1)):
            far = (j if way == 0 else 4 - j) if j else 4
            k = lax.rem(z - sign * far + NZ, NZ)
            lists.append((k // 4, walk(k, way, far)))
        for q, (reach, side, e) in enumerate(here):
            if j:
                back = side == lists[1][0]
                groups = [
                    (jnp.where(back, gb[0], gf[0]), jnp.where(back, gb[1], gf[1]))
                    for gf, gb in zip(*[pad(groups) for _, groups in lists])
                ]
                place, found = locate(e, groups)
                flag = jnp.where(back, 1, 0)
            else:
                k, groups = lists[(q // 2) % 2]
                place, found = locate(e, groups)
                flag = jnp.where(side == k, 1, 0)
                place = jnp.where(flag > 0, place, e)
            tab[64 + j * 8 + q] = place
            tab[96 + j * 8 + q] = flag


def pad(groups):
    return groups + [(jnp.int32(0), jnp.int32(0))] * (4 - len(groups))


def segments(caps):
    p1, p2, p3, p4 = caps
    head = [
        (1, 0, p4), (1, p4, p3), (2, 0, p4), (1, p3, p2), (3, 0, p4),
        (2, p4, p3), (4, 0, p4), (2, p3, p2),
    ]
    near, far = (1, p2, p1), (3, p4, p3)
    return [[piece for piece in order if piece[1] < piece[2]] for order in (head + [near, far], head + [far, near])]


def whole_kernel(
    caps, tab, pool, fresh, q, out, dev,
    qx, fx, poolbuf, stage, r1, r2, r3, r4, yst, ctx,
    qs, kt, vs, top, acc, ost, devp, gathered,
    zsend, zrecv, ysend, yrecv, xsend, xrecv, lsem, dsend, drecv, osend, orecv,
):
    s = lax.axis_index("seq")
    x = lax.axis_index("tp")
    me = lax.axis_index("req")
    z, y = me // NY, lax.rem(me, NY)
    p1, p2, p3, p4 = caps
    zdev = [(s, x, lax.rem(z + 1, NZ) * NY + y), (s, x, lax.rem(z + NZ - 1, NZ) * NY + y)]
    ydev = [(s, x, z * NY + lax.rem(y + dy, NY)) for dy in (1, 2, 3)]
    peers = [(lax.rem(s + ds, 2), lax.rem(x + dx, 4), me) for ds in range(2) for dx in range(4)][1:]
    core = peers[3]

    barrier = pltpu.get_barrier_semaphore()
    for device in peers + zdev + ydev:
        pl.semaphore_signal(barrier, inc=1, device_id=device, device_id_type=MESH)
    pl.semaphore_wait(barrier, len(peers + zdev + ydev))

    other = pl.ds(pl.multiple_of((1 - s) * HCOLS, HCOLS), HCOLS)
    mine = pl.ds(pl.multiple_of(s * HCOLS, HCOLS), HCOLS)
    swaps = [(pool.at[1 - s], poolbuf.at[s]), (q.at[:, other], qx.at[s]), (fresh.at[1 - s], fx.at[s])]
    keeps = [(pool.at[s], poolbuf.at[s]), (q.at[:, mine], qx.at[s]), (fresh.at[s], fx.at[s])]
    swaps = [
        pltpu.make_async_remote_copy(
            src_ref=src, dst_ref=dst, send_sem=xsend.at[i], recv_sem=xrecv.at[i],
            device_id=core, device_id_type=MESH,
        )
        for i, (src, dst) in enumerate(swaps)
    ]
    keeps = [pltpu.make_async_copy(src, dst, lsem.at[i]) for i, (src, dst) in enumerate(keeps)]
    for i in range(3):
        swaps[i].start()
        keeps[i].start()
    keeps[0].wait()
    swaps[0].wait()

    buffers = [
        [(stage.at[0], 0), (r1, 0), (r2, 0), (r3, 0), (r4, 0)],
        [(stage.at[1], 0), (r3, p3), (r2, p2), (r1, p1), (r4, p4)],
    ]
    orders = segments(caps)
    index = [{piece: i for i, piece in enumerate(order)} for order in orders]

    def zcopy(way, piece):
        hop, low, high = piece
        src, src_at = buffers[way][hop - 1]
        dst, dst_at = buffers[way][hop]
        i = index[way][piece]
        return pltpu.make_async_remote_copy(
            src_ref=src.at[pl.ds(src_at + low, high - low)],
            dst_ref=dst.at[pl.ds(dst_at + low, high - low)],
            send_sem=zsend.at[way, i],
            recv_sem=zrecv.at[way, i],
            device_id=zdev[way],
            device_id_type=MESH,
        )

    for step in range(len(orders[0])):
        for way in range(2):
            hop, low, high = piece = orders[way][step]
            if hop == 1:

                def fetch(place, carry):
                    row = tab[way * 32 + place]
                    stage[way, place] = poolbuf[row // NT, lax.rem(row, NT)]
                    return carry

                lax.fori_loop(low, high, fetch, 0)
            else:
                zcopy(way, (hop - 1, low, high)).wait_recv()
            zcopy(way, piece).start()
        if step == 2:
            for i in (1, 2):
                keeps[i].wait()
                swaps[i].wait()
            eye = jnp.where(
                lax.broadcasted_iota(jnp.int32, (TILE, TILE), 0)
                == lax.broadcasted_iota(jnp.int32, (TILE, TILE), 1),
                1.0,
                0.0,
            ).astype(jnp.bfloat16)
            for slot in range(2):

                def lay(g, carry):
                    rows = pl.ds(pl.multiple_of(g * TILE, TILE), TILE)
                    qs[slot, rows, :HD] = qx[slot, :, rows]
                    qs[slot, rows, HD:] = eye
                    return carry

                lax.fori_loop(0, PER_KV, lay, 0)
            vs[...] = jnp.ones(vs.shape, vs.dtype)
            top[...] = jnp.full(top.shape, LOW, top.dtype)
            acc[...] = jnp.zeros(acc.shape, acc.dtype)

    def group(j):
        return lax.rem(z - j + NZ, 4)

    def ycopy(j, dy):
        return pltpu.make_async_remote_copy(
            src_ref=yst.at[j, dy - 1],
            dst_ref=ctx.at[NY * group(j) + y],
            send_sem=ysend.at[j, dy - 1],
            recv_sem=yrecv.at[j, dy - 1],
            device_id=ydev[dy - 1],
            device_id_type=MESH,
        )

    def hand_out(j):
        for way in range(2):
            last = [(4, 0, p4), (1, p2, p1), (2, p3, p2), (3, p4, p3)]
            piece = last[j if way == 0 else (4 - j) % 4]
            if piece in index[way]:
                zcopy(way, piece).wait_recv()

        def picked(column, c):
            at = j * 8 + column * 2 + c
            place, side = tab[64 + at], tab[96 + at]
            if j:
                return (r1, r2, r3)[j - 1][place + side * caps[j - 1]]
            near = jnp.where(side > 0, 0, place)
            far = jnp.where(side > 0, place, 0)
            far = far + lax.rem(column, 2) * p4
            local = poolbuf[near // NT, lax.rem(near, NT)]
            return jnp.where(side > 0, r4[far], local)

        for dy in (2, 1, 3):
            column = lax.rem(y + dy, NY)
            for c in range(2):
                yst[j, dy - 1, c] = picked(column, c)
            ycopy(j, dy).start()
        for c in range(2):
            ctx[NY * group(j) + y, c] = picked(y, c)

    def arrived(j):
        for dy in (1, 2, 3):
            ycopy(j, dy).wait_recv()

    def attend(j):
        for c in range(2):
            entry = tab[128 + c]
            last = jnp.maximum(entry, 0) * TILE + lax.broadcasted_iota(jnp.int32, (TILE, TILE), 0)
            for i in range(NY):
                t = NY * group(j) + i
                tile = jnp.where(t == entry, fx[c], ctx[t, c])
                cols = slice(i * TILE, (i + 1) * TILE)
                kt[c, :HD, cols] = jnp.transpose(tile[:, :HD])
                vs[c, cols, HD:] = tile[:, HD:]
                at = t * TILE + lax.broadcasted_iota(jnp.int32, (TILE, TILE), 1)
                kt[c, HD:, cols] = jnp.where(at <= last, 0.0, LOW).astype(jnp.bfloat16)
        for slot in range(2):

            def block(i, carry):
                rows = pl.ds(pl.multiple_of(i * 2 * TILE, 2 * TILE), 2 * TILE)
                qq = qs[slot, rows]
                parts = [jnp.dot(qq, kt[slot], preferred_element_type=jnp.float32)]
                if slot:
                    parts.append(jnp.dot(qq[:, :HD], kt[0, :HD], preferred_element_type=jnp.float32))
                peak = functools.reduce(
                    jnp.maximum, [part[:, i * HD : (i + 1) * HD] for part in parts for i in range(NY)]
                )
                old = top[slot, rows]
                new = jnp.maximum(old, jnp.max(peak, axis=1, keepdims=True))
                top[slot, rows] = new
                wide = jnp.concatenate([new] * NY, axis=1)
                factor = jnp.exp2((old - new) * SCALE)
                total = acc[slot, rows] * jnp.concatenate([factor, factor], axis=1)
                for part, c in zip(parts, (slot, 0)):
                    weights = jnp.exp2((part - wide) * SCALE).astype(jnp.bfloat16)
                    total = total + jnp.dot(weights, vs[c], preferred_element_type=jnp.float32)
                acc[slot, rows] = total
                return carry

            lax.fori_loop(0, PER_KV // 2, block, 0, unroll=3)

    sends = [
        pltpu.make_async_remote_copy(
            src_ref=devp, dst_ref=gathered.at[i], send_sem=dsend.at[i], recv_sem=drecv.at[i],
            device_id=device, device_id_type=MESH,
        )
        for i, device in enumerate(peers)
    ]

    def turn(i, carry):
        j = lax.rem(i, 2) * 2 + i // 2

        @pl.when(i == 1)
        def _():
            hand_out(3)

        arrived(j)

        @pl.when(i == 3)
        def _():
            devp[...] = jnp.zeros(devp.shape, devp.dtype)
            for c in range(2):
                entry = tab[128 + c]
                gap = fx[c].astype(jnp.float32) - ctx[jnp.maximum(entry, 0), c].astype(jnp.float32)
                gap = gap * gap
                gap = jnp.transpose(gap[:, :HD] + gap[:, HD:])
                total = jnp.sum(gap, axis=0, keepdims=True) / (2 * KVH * HD)
                devp[c : c + 1] = jnp.where(entry >= 0, total, 0.0)
            for send in sends:
                send.start()

        attend(j)
        return carry

    hand_out(0)
    hand_out(2)
    hand_out(1)
    lax.fori_loop(0, 4, turn, 0)

    def result(slot, g):
        part = acc[slot, pl.ds(pl.multiple_of(g * TILE, TILE), TILE)]
        ratio = part[:, HD:] / part[:, :HD]
        return jnp.where(tab[128 + slot] >= 0, ratio, 0.0).astype(jnp.bfloat16)

    def put_other(g, carry):
        ost[:, pl.ds(pl.multiple_of(g * HD, HD), HD)] = result(1 - s, g)
        return carry

    def put_mine(g, carry):
        out[:, pl.ds(pl.multiple_of(s * HCOLS + g * HD, HD), HD)] = result(s, g)
        return carry

    lax.fori_loop(0, PER_KV, put_other, 0, unroll=2)
    swap = pltpu.make_async_remote_copy(
        src_ref=ost, dst_ref=out.at[:, mine], send_sem=osend, recv_sem=orecv,
        device_id=core, device_id_type=MESH,
    )
    swap.start()
    lax.fori_loop(0, PER_KV, put_mine, 0, unroll=2)

    total = devp[...]
    for i in range(7):
        sends[i].wait()
        total = total + gathered[i]
    dev[...] = jnp.where(s == 0, total[0:1], total[1:2])
    for j in range(4):
        for dy in (1, 2, 3):
            ycopy(j, dy).wait_send()
    for way in range(2):
        for piece in orders[way]:
            zcopy(way, piece).wait_send()
    swap.wait()


def whole_call(level, tab, pool, fresh, q):
    caps = LEVELS[level]
    p1, p2, p3, p4 = caps
    tile = (TILE, 2 * HD)
    bf = jnp.bfloat16
    anyspace = pl.BlockSpec(memory_space=pl.ANY)
    smem = pl.BlockSpec(memory_space=pltpu.SMEM)
    vmem = pl.BlockSpec(memory_space=pltpu.VMEM)
    dma = pltpu.SemaphoreType.DMA
    return pl.pallas_call(
        functools.partial(whole_kernel, caps),
        out_shape=(
            jax.ShapeDtypeStruct((TILE, 2 * HCOLS), bf),
            jax.ShapeDtypeStruct((1, TILE), jnp.float32),
        ),
        in_specs=[smem, anyspace, anyspace, anyspace],
        out_specs=(vmem, vmem),
        scratch_shapes=[
            pltpu.VMEM((2, TILE, HCOLS), bf),
            pltpu.VMEM((2,) + tile, bf),
            pltpu.VMEM((2, NT) + tile, bf),
            pltpu.VMEM((2, p1) + tile, bf),
            pltpu.VMEM((p1 + p3,) + tile, bf),
            pltpu.VMEM((2 * p2,) + tile, bf),
            pltpu.VMEM((p3 + p1,) + tile, bf),
            pltpu.VMEM((2 * p4,) + tile, bf),
            pltpu.VMEM((4, 3, 2) + tile, bf),
            pltpu.VMEM((NT, 2) + tile, bf),
            pltpu.VMEM((2, HCOLS, 2 * HD), bf),
            pltpu.VMEM((2, 2 * HD, NY * TILE), bf),
            pltpu.VMEM((2, NY * TILE, 2 * HD), bf),
            pltpu.VMEM((2, HCOLS, HD), jnp.float32),
            pltpu.VMEM((2, HCOLS, 2 * HD), jnp.float32),
            pltpu.VMEM((TILE, HCOLS), bf),
            pltpu.VMEM((8, TILE), jnp.float32),
            pltpu.VMEM((7, 8, TILE), jnp.float32),
            dma((2, 10)),
            dma((2, 10)),
            dma((4, 3)),
            dma((4, 3)),
            dma((3,)),
            dma((3,)),
            dma((3,)),
            dma((7,)),
            dma((7,)),
            dma,
            dma,
        ],
        compiler_params=pltpu.CompilerParams(
            collective_id=level, has_side_effects=True, vmem_limit_bytes=52 * 2**20
        ),
    )(tab, pool, fresh, q)


def on_device(cache_pool, fresh_kv, queries, stretch_owner, stretch_slot, recomp):
    smem = pl.BlockSpec(memory_space=pltpu.SMEM)
    word = jnp.int32
    tab, level = pl.pallas_call(
        prepare_kernel,
        out_shape=(jax.ShapeDtypeStruct((131,), word), jax.ShapeDtypeStruct((1,), word)),
        in_specs=[smem] * 3,
        out_specs=(smem, smem),
        scratch_shapes=[pltpu.SMEM((128,), word)] * 2,
    )(*(jnp.transpose(a.reshape(-1, 2)) for a in (stretch_owner, stretch_slot, recomp)))
    out, dev = lax.switch(
        level[0],
        [functools.partial(whole_call, i) for i in range(len(LEVELS))],
        tab, cache_pool[0, 0], fresh_kv[0], queries[0],
    )
    return out[None], dev


def solution(mesh):
    placed = (
        P("seq", "req", "tp", None, None, None),
        P("req", "tp", "seq", None),
        P("req", "seq", "tp"),
        P(),
        P(),
        P(),
    )
    return jax.shard_map(
        on_device,
        mesh=mesh,
        in_specs=placed,
        out_specs=(P("req", "seq", "tp"), P("req", "seq")),
        check_vma=False,
    )
```

profile of v0, /device:TPU:1, one launch (start us, length us, event | category | flops | bytes accessed | tf_op | source)
XLA Modules:
  0.0 90.2 jit_solution(11013739986638938904)
XLA Ops:
  0.6 6.1 %shard_map.77 = (s32[131]{0:T(256)S(1)}, s32[1]{0:T(128)}) custom-call(s32[2,32]{1,0:T(2,128)} %bitcast.29, s32[2,32]{1,0:T(2,128)} %bitcast.30, s32[2,32]{1,0:T(2,128)} %bitcast.31), custom_call_target="tpu_custom_call" | custom-call | tf_op jit(solution)/shard_map/pallas_call | solution.py:463
  7.4 81.4 %conditional.1 = (f32[1,128]{1,0:T(1,128)S(1)}, bf16[1,128,3072]{2,1,0:T(8,128)(2,1)S(1)}) conditional(s32[]{:T(128)} %bitcast.8, (s32[131]{0:T(256)S(1)}, bf16[2,16,128,256]{3,2,1,0:T(8,128)(2,1)}, bf16[2,128,256]{2,1,0:T(8,128)(2,1)}, bf16[128,3072]{1,0:T(8,128)(2,1)}) %tuple.44, (s32[131]{0:T(256)S(1)}, ...), branch_computations={%region_0.0_spmd, %region_1.0_spmd, %region_2.0_spmd, %region_3.0_... | conditional | bytes 16 | solution.py:470
  7.4 81.1 %branch_1_fun.1 = (bf16[128,3072]{1,0:T(8,128)(2,1)S(1)}, f32[1,128]{1,0:T(1,128)S(1)}) custom-call(s32[131]{0:T(256)S(1)} %get-tuple-element.47.tab, bf16[2,16,128,256]{3,2,1,0:T(8,128)(2,1)} %get-tuple-element.48.pool, bf16[2,128,256]{2,1,0:T(8,128)(2,1)} %get-tuple-element.49.fresh, bf16[128,3072]{1,0:T(8,128)(2,1)} %get-tuple-element.50.q), custom_call_target="tpu_custom_call" | custom-call | tf_op jit(solution)/shard_map/cond/branch_1_fun/pallas_call | solution.py:415
  88.8 0.9 copy.18
  89.7 0.5 copy.19
where the time goes:
time: 90.3 us; the launch traced here: 90.2 us
  Pallas kernels  87.3 us (97%)
  local copies, waits for them, and re-layouts  1.39 us (2%)
  between operations  1.3 us (1%)
    pallas_call x1, Pallas kernels, whole_call(): pl.pallas_call(functools.partial(whole_kernel, caps), out_shape=(jax.Shap...  81.1 us
    pallas_call x1, Pallas kernels, on_device(): pl.pallas_call(prepare_kernel, out_shape=(jax.ShapeDtypeStruct((131,), wo...  6.12 us

commit v1 on v0

v1 whole, which is shorter than its diff:
```python
import functools

import jax
import jax.numpy as jnp
from jax import lax
from jax.experimental import pallas as pl
from jax.experimental.pallas import tpu as pltpu
from jax.sharding import PartitionSpec as P

KVH = 8
HD = 128
TILE = 128
NT = 16
PER_KV = 12
HCOLS = PER_KV * HD
NZ = 8
NY = 4
MESH = pl.DeviceIdType.MESH
SCALE = HD**-0.5 * 1.4426950408889634
LOW = -1e30
LEVELS = ((11, 8, 5, 3), (12, 9, 6, 3), (13, 10, 7, 4), (15, 12, 9, 4), (28, 20, 12, 4))


def bits_set(word):
    shift = lax.shift_right_logical
    word = word - (shift(word, 1) & 0x55555555)
    word = (word & 0x33333333) + (shift(word, 2) & 0x33333333)
    word = (word + shift(word, 4)) & 0x0F0F0F0F
    word = word + shift(word, 8)
    return (word + shift(word, 16)) & 63


def prepare_kernel(
    owner, slot, recomp, pool, fresh, q, tab, level, poolx, fx, qx, sets, flips, send_sem, recv_sem
):
    s = lax.axis_index("seq")
    me = lax.axis_index("req")
    z, y = me // NY, lax.rem(me, NY)
    core = (1 - s, lax.axis_index("tp"), me)
    barrier = pltpu.get_barrier_semaphore()
    pl.semaphore_signal(barrier, inc=1, device_id=core, device_id_type=MESH)
    pl.semaphore_wait(barrier, 1)
    other = pl.ds(pl.multiple_of((1 - s) * HCOLS, HCOLS), HCOLS)
    swaps = [
        pltpu.make_async_remote_copy(
            src_ref=src, dst_ref=dst, send_sem=send_sem.at[i], recv_sem=recv_sem.at[i],
            device_id=core, device_id_type=MESH,
        )
        for i, (src, dst) in enumerate(((pool.at[1 - s], poolx), (fresh.at[1 - s], fx), (q.at[:, other], qx)))
    ]
    for swap in swaps:
        swap.start()

    def passage(r, c):
        block = owner[c, r] // NT
        side = lax.rem(block, 2)
        first, second = recomp[0, r], recomp[1, r]
        second = jnp.maximum(second + 1, 0)
        reach = second if c else jnp.where(second > 0, NT, jnp.maximum(first + 1, 0))
        return reach, side, (block // 2) * NT + slot[c, r]

    def read(row, carry):
        words = {}
        for q in range(2 * NY):
            reach, side, e = passage(row * NY + q // 2, q % 2)
            bit = jnp.left_shift(1, e)
            low = jnp.where(side == 0, bit, 0)
            for group in range(4):
                wanted = reach > NY * group
                for k, part in ((group, low), (group + 4, bit ^ low)):
                    key = (k, (q // 2) % 2)
                    part = jnp.where(wanted, part, 0)
                    words[key] = words[key] | part if key in words else part
        for (k, odd), word in words.items():
            sets[(k * NZ + row) * 2 + odd] = word
        return carry

    lax.fori_loop(0, NZ, read, 0)

    def needs(k, d, way):
        at = (k * NZ + lax.rem(k + (d if way == 0 else -d) + NZ, NZ)) * 2
        return sets[at + (way ^ flips[k])] if d == 4 else sets[at] | sets[at + 1]

    def count(k, most):
        far = (k * NZ + lax.rem(k + 4, NZ)) * 2
        near = [[needs(k, d, way) for d in (3, 2, 1)] for way in range(2)]
        found, totals = [], []
        for flip in range(2):
            sizes = []
            for way in range(2):
                seen = sets[far + (way ^ flip)]
                sizes.append([bits_set(seen)])
                for more in near[way]:
                    seen = seen | more
                    sizes[way].append(bits_set(seen))
            found.append([jnp.maximum(a, b) for a, b in zip(*sizes)])
            totals.append(sum(found[flip]))
        flip = totals[1] < totals[0]
        flips[k] = jnp.where(flip, 1, 0)
        return tuple(jnp.maximum(m, jnp.where(flip, b, a)) for m, a, b in zip(most, *found))

    most = lax.fori_loop(0, NZ, count, (jnp.int32(0),) * 4)
    pick = jnp.int32(0)
    for caps in LEVELS[:-1]:
        over = functools.reduce(jnp.logical_or, [m > cap for m, cap in zip(most, caps[::-1])])
        pick = pick + jnp.where(over, 1, 0)
    level[0] = pick

    def walk(k, way, far):
        seen, groups = jnp.int32(0), []
        for d in range(4, far - 1, -1):
            wanted = needs(k, d, way)
            groups.append((wanted & ~seen, bits_set(seen)))
            seen = seen | wanted
        return groups

    def listed(place, ways):
        out = []
        for way, words in enumerate(ways):
            head = jnp.int32(0)
            for word in words[::-1]:
                head = jnp.where(word != 0, word, head)
            low = head & -head
            tab[way * 32 + place] = bits_set(low - 1) & 31
            out.append(tuple(word & ~low for word in words))
        return tuple(out)

    lax.fori_loop(
        0, LEVELS[-1][0], listed, tuple(tuple(g[0] for g in walk(z, way, 1)) for way in range(2)), unroll=2
    )
    for c in range(2):
        tab[128 + c] = recomp[c, me]
    tab[130] = flips[lax.rem(z + 4, NZ)]
    here = [passage(me - y + q // 2, q % 2) for q in range(2 * NY)]
    for j in range(4):
        lists = []
        for way, sign in ((0, 1), (1, -1)):
            far = (j if way == 0 else 4 - j) if j else 4
            k = lax.rem(z - sign * far + NZ, NZ)
            lists.append((k // 4, walk(k, way, far)))
        for q, (reach, side, e) in enumerate(here):
            back = side == lists[1][0]
            if j == 0:
                k = lax.rem(z + 4, NZ)
                groups = [(sets[(k * NZ + z) * 2 + (q // 2) % 2], jnp.int32(0))]
            else:
                groups = [
                    (jnp.where(back, gb[0], gf[0]), jnp.where(back, gb[1], gf[1]))
                    for gf, gb in zip(*[pad(groups) for _, groups in lists])
                ]
            bit = jnp.left_shift(1, e)
            word, base = jnp.int32(0), jnp.int32(0)
            for new, start in groups:
                has = (new & bit) != 0
                word, base = jnp.where(has, new, word), jnp.where(has, start, base)
            place = jnp.where(word != 0, base + bits_set(word & (bit - 1)), 0)
            if not j:
                place = jnp.where(back, place, e)
            tab[64 + j * 8 + q] = place
            tab[96 + j * 8 + q] = jnp.where(back, 1, 0)
    for swap in swaps:
        swap.wait()


def pad(groups):
    return groups + [(jnp.int32(0), jnp.int32(0))] * (4 - len(groups))


def prepare_call(owner, slot, recomp, pool, fresh, q):
    smem = pl.BlockSpec(memory_space=pltpu.SMEM)
    anyspace = pl.BlockSpec(memory_space=pl.ANY)
    word, bf = jnp.int32, jnp.bfloat16
    return pl.pallas_call(
        prepare_kernel,
        out_shape=(
            jax.ShapeDtypeStruct((131,), word),
            jax.ShapeDtypeStruct((1,), word),
            jax.ShapeDtypeStruct((NT, TILE, 2 * HD), bf),
            jax.ShapeDtypeStruct((TILE, 2 * HD), bf),
            jax.ShapeDtypeStruct((TILE, HCOLS), bf),
        ),
        in_specs=[smem] * 3 + [anyspace] * 3,
        out_specs=(smem, smem, anyspace, anyspace, anyspace),
        scratch_shapes=[
            pltpu.SMEM((128,), word),
            pltpu.SMEM((NZ,), word),
            pltpu.SemaphoreType.DMA((3,)),
            pltpu.SemaphoreType.DMA((3,)),
        ],
        compiler_params=pltpu.CompilerParams(collective_id=len(LEVELS), has_side_effects=True),
    )(owner, slot, recomp, pool, fresh, q)


def segments(caps):
    p1, p2, p3, p4 = caps
    head = [
        (1, 0, p4), (1, p4, p3), (2, 0, p4), (1, p3, p2), (3, 0, p4),
        (2, p4, p3), (4, 0, p4), (2, p3, p2),
    ]
    near, far = (1, p2, p1), (3, p4, p3)
    return [[piece for piece in order if piece[1] < piece[2]] for order in (head + [near, far], head + [far, near])]


def whole_kernel(
    caps, tab, pool, fresh, q, poolin, fin, qin, out, dev,
    qx, fx, poolbuf, stage, r1, r2, r3, r4, yst, ctx,
    qs, kt, vs, top, acc, ost, devp, gathered,
    zsend, zrecv, ysend, yrecv, lsem, dsend, drecv, osend, orecv,
):
    s = lax.axis_index("seq")
    x = lax.axis_index("tp")
    me = lax.axis_index("req")
    z, y = me // NY, lax.rem(me, NY)
    p1, p2, p3, p4 = caps
    zdev = [(s, x, lax.rem(z + 1, NZ) * NY + y), (s, x, lax.rem(z + NZ - 1, NZ) * NY + y)]
    ydev = [(s, x, z * NY + lax.rem(y + dy, NY)) for dy in (1, 2, 3)]
    peers = [(lax.rem(s + ds, 2), lax.rem(x + dx, 4), me) for ds in range(2) for dx in range(4)][1:]
    core = peers[3]

    mine = pl.ds(pl.multiple_of(s * HCOLS, HCOLS), HCOLS)
    loads = [
        pltpu.make_async_copy(src, dst, lsem.at[i])
        for i, (src, dst) in enumerate(
            (
                (pool.at[s], poolbuf.at[s]),
                (poolin, poolbuf.at[1 - s]),
                (fresh.at[s], fx.at[s]),
                (fin, fx.at[1 - s]),
                (q.at[:, mine], qx.at[s]),
                (qin, qx.at[1 - s]),
            )
        )
    ]
    for load in loads:
        load.start()
    barrier = pltpu.get_barrier_semaphore()
    for device in peers + zdev + ydev:
        pl.semaphore_signal(barrier, inc=1, device_id=device, device_id_type=MESH)
    loads[0].wait()
    loads[1].wait()
    pl.semaphore_wait(barrier, len(peers + zdev + ydev))

    buffers = [
        [(stage.at[0], 0), (r1, 0), (r2, 0), (r3, 0), (r4, 0)],
        [(stage.at[1], 0), (r3, p3), (r2, p2), (r1, p1), (r4, p4)],
    ]
    orders = segments(caps)
    index = [{piece: i for i, piece in enumerate(order)} for order in orders]

    def zcopy(way, piece):
        hop, low, high = piece
        src, src_at = buffers[way][hop - 1]
        dst, dst_at = buffers[way][hop]
        i = index[way][piece]
        return pltpu.make_async_remote_copy(
            src_ref=src.at[pl.ds(src_at + low, high - low)],
            dst_ref=dst.at[pl.ds(dst_at + low, high - low)],
            send_sem=zsend.at[way, i],
            recv_sem=zrecv.at[way, i],
            device_id=zdev[way],
            device_id_type=MESH,
        )

    for step in range(len(orders[0])):
        for way in range(2):
            hop, low, high = piece = orders[way][step]
            if hop == 1:

                def fetch(place, carry):
                    row = tab[way * 32 + place]
                    stage[way, place] = poolbuf[row // NT, lax.rem(row, NT)]
                    return carry

                lax.fori_loop(low, high, fetch, 0)
            else:
                zcopy(way, (hop - 1, low, high)).wait_recv()
            zcopy(way, piece).start()
        if step == 2:
            for load in loads[2:]:
                load.wait()
            eye = jnp.where(
                lax.broadcasted_iota(jnp.int32, (TILE, TILE), 0)
                == lax.broadcasted_iota(jnp.int32, (TILE, TILE), 1),
                1.0,
                0.0,
            ).astype(jnp.bfloat16)
            for slot in range(2):

                def lay(g, carry):
                    rows = pl.ds(pl.multiple_of(g * TILE, TILE), TILE)
                    qs[slot, rows, :HD] = qx[slot, :, rows]
                    qs[slot, rows, HD:] = eye
                    return carry

                lax.fori_loop(0, PER_KV, lay, 0)
            vs[...] = jnp.ones(vs.shape, vs.dtype)
            top[...] = jnp.full(top.shape, LOW, top.dtype)
            acc[...] = jnp.zeros(acc.shape, acc.dtype)

    def group(j):
        return lax.rem(z - j + NZ, 4)

    def ycopy(j, dy):
        return pltpu.make_async_remote_copy(
            src_ref=yst.at[j, dy - 1],
            dst_ref=ctx.at[NY * group(j) + y],
            send_sem=ysend.at[j, dy - 1],
            recv_sem=yrecv.at[j, dy - 1],
            device_id=ydev[dy - 1],
            device_id_type=MESH,
        )

    def hand_out(j):
        for way in range(2):
            last = [(4, 0, p4), (1, p2, p1), (2, p3, p2), (3, p4, p3)]
            piece = last[j if way == 0 else (4 - j) % 4]
            if piece in index[way]:
                zcopy(way, piece).wait_recv()

        def picked(column, c):
            at = j * 8 + column * 2 + c
            place, side = tab[64 + at], tab[96 + at]
            if j:
                return (r1, r2, r3)[j - 1][place + side * caps[j - 1]]
            near = jnp.where(side > 0, 0, place)
            far = jnp.where(side > 0, place, 0)
            far = far + (lax.rem(column, 2) ^ tab[130]) * p4
            local = poolbuf[near // NT, lax.rem(near, NT)]
            return jnp.where(side > 0, r4[far], local)

        for dy in (2, 1, 3):
            column = lax.rem(y + dy, NY)

            def give(c, carry):
                yst[j, dy - 1, c] = picked(column, c)
                return carry

            lax.fori_loop(0, 2, give, 0)
            ycopy(j, dy).start()

        def keep(c, carry):
            ctx[NY * group(j) + y, c] = picked(y, c)
            return carry

        lax.fori_loop(0, 2, keep, 0)

    def arrived(j):
        for dy in (1, 2, 3):
            ycopy(j, dy).wait_recv()

    def attend(j):
        for c in range(2):
            entry = tab[128 + c]
            last = jnp.maximum(entry, 0) * TILE + lax.broadcasted_iota(jnp.int32, (TILE, TILE), 0)

            def blend(i, carry):
                t = NY * group(j) + i
                tile = jnp.where(t == entry, fx[c], ctx[t, c])
                cols = pl.ds(pl.multiple_of(i * TILE, TILE), TILE)
                kt[c, :HD, cols] = jnp.transpose(tile[:, :HD])
                vs[c, cols, HD:] = tile[:, HD:]
                at = t * TILE + lax.broadcasted_iota(jnp.int32, (TILE, TILE), 1)
                kt[c, HD:, cols] = jnp.where(at <= last, 0.0, LOW).astype(jnp.bfloat16)
                return carry

            lax.fori_loop(0, NY, blend, 0, unroll=2)

    def update(slot, i):
        rows = pl.ds(pl.multiple_of(i * 2 * TILE, 2 * TILE), 2 * TILE)
        qq = qs[slot, rows]
        parts = [jnp.dot(qq, kt[slot], preferred_element_type=jnp.float32)]
        if slot:
            parts.append(jnp.dot(qq[:, :HD], kt[0, :HD], preferred_element_type=jnp.float32))
        peak = functools.reduce(
            jnp.maximum, [part[:, i * HD : (i + 1) * HD] for part in parts for i in range(NY)]
        )
        old = top[slot, rows]
        new = jnp.maximum(old, jnp.max(peak, axis=1, keepdims=True))
        top[slot, rows] = new
        wide = jnp.concatenate([new] * NY, axis=1)
        factor = jnp.exp2((old - new) * SCALE)
        total = acc[slot, rows] * jnp.concatenate([factor, factor], axis=1)
        for part, c in zip(parts, (slot, 0)):
            weights = jnp.exp2((part - wide) * SCALE).astype(jnp.bfloat16)
            total = total + jnp.dot(weights, vs[c], preferred_element_type=jnp.float32)
        acc[slot, rows] = total

    def result(slot, g):
        part = acc[slot, pl.ds(pl.multiple_of(g * TILE, TILE), TILE)]
        ratio = part[:, HD:] / part[:, :HD]
        return jnp.where(tab[128 + slot] >= 0, ratio, 0.0).astype(jnp.bfloat16)

    span = 4 * HD

    def swap(part):
        return pltpu.make_async_remote_copy(
            src_ref=ost.at[:, pl.ds(pl.multiple_of(part * span, span), span)],
            dst_ref=out.at[:, pl.ds(pl.multiple_of(s * HCOLS + part * span, span), span)],
            send_sem=osend.at[part],
            recv_sem=orecv.at[part],
            device_id=core,
            device_id_type=MESH,
        )

    sends = [
        pltpu.make_async_remote_copy(
            src_ref=devp, dst_ref=gathered.at[i], send_sem=dsend.at[i], recv_sem=drecv.at[i],
            device_id=device, device_id_type=MESH,
        )
        for i, device in enumerate(peers)
    ]

    def turn(i, carry):
        j = lax.rem(i, 2) * 2 + i // 2

        @pl.when(i == 1)
        def _():
            hand_out(3)

        arrived(j)

        @pl.when(i == 3)
        def _():
            devp[...] = jnp.zeros(devp.shape, devp.dtype)
            for c in range(2):
                entry = tab[128 + c]
                gap = fx[c].astype(jnp.float32) - ctx[jnp.maximum(entry, 0), c].astype(jnp.float32)
                gap = gap * gap
                gap = jnp.transpose(gap[:, :HD] + gap[:, HD:])
                total = jnp.sum(gap, axis=0, keepdims=True) / (2 * KVH * HD)
                devp[c : c + 1] = jnp.where(entry >= 0, total, 0.0)
            for send in sends:
                send.start()

        attend(j)

        def heads(part, carry):
            for slot in range(2):
                for n in range(2):
                    update(slot, part * 2 + n)

            @pl.when(i == 3)
            def _():
                def put(n, carry):
                    g = part * 4 + n
                    cols = pl.ds(pl.multiple_of(g * HD, HD), HD)
                    ost[:, cols] = result(1 - s, g)
                    out[:, pl.ds(pl.multiple_of(s * HCOLS + g * HD, HD), HD)] = result(s, g)
                    return carry

                lax.fori_loop(0, 4, put, 0)
                swap(part).start()

            return carry

        lax.fori_loop(0, PER_KV // 4, heads, 0)
        return carry

    hand_out(0)
    hand_out(2)
    hand_out(1)
    lax.fori_loop(0, 4, turn, 0)

    total = devp[...]
    for i in range(7):
        sends[i].wait()
        total = total + gathered[i]
    dev[...] = jnp.where(s == 0, total[0:1], total[1:2])
    for j in range(4):
        for dy in (1, 2, 3):
            ycopy(j, dy).wait_send()
    for way in range(2):
        for piece in orders[way]:
            zcopy(way, piece).wait_send()
    for part in range(PER_KV // 4):
        swap(part).wait()


def whole_call(level, *args):
    caps = LEVELS[level]
    p1, p2, p3, p4 = caps
    tile = (TILE, 2 * HD)
    bf = jnp.bfloat16
    anyspace = pl.BlockSpec(memory_space=pl.ANY)
    smem = pl.BlockSpec(memory_space=pltpu.SMEM)
    vmem = pl.BlockSpec(memory_space=pltpu.VMEM)
    dma = pltpu.SemaphoreType.DMA
    return pl.pallas_call(
        functools.partial(whole_kernel, caps),
        out_shape=(
            jax.ShapeDtypeStruct((TILE, 2 * HCOLS), bf),
            jax.ShapeDtypeStruct((1, TILE), jnp.float32),
        ),
        in_specs=[smem] + [anyspace] * 6,
        out_specs=(vmem, vmem),
        scratch_shapes=[
            pltpu.VMEM((2, TILE, HCOLS), bf),
            pltpu.VMEM((2,) + tile, bf),
            pltpu.VMEM((2, NT) + tile, bf),
            pltpu.VMEM((2, p1) + tile, bf),
            pltpu.VMEM((p1 + p3,) + tile, bf),
            pltpu.VMEM((2 * p2,) + tile, bf),
            pltpu.VMEM((p3 + p1,) + tile, bf),
            pltpu.VMEM((2 * p4,) + tile, bf),
            pltpu.VMEM((4, 3, 2) + tile, bf),
            pltpu.VMEM((NT, 2) + tile, bf),
            pltpu.VMEM((2, HCOLS, 2 * HD), bf),
            pltpu.VMEM((2, 2 * HD, NY * TILE), bf),
            pltpu.VMEM((2, NY * TILE, 2 * HD), bf),
            pltpu.VMEM((2, HCOLS, HD), jnp.float32),
            pltpu.VMEM((2, HCOLS, 2 * HD), jnp.float32),
            pltpu.VMEM((TILE, HCOLS), bf),
            pltpu.VMEM((8, TILE), jnp.float32),
            pltpu.VMEM((7, 8, TILE), jnp.float32),
            dma((2, 10)),
            dma((2, 10)),
            dma((4, 3)),
            dma((4, 3)),
            dma((6,)),
            dma((7,)),
            dma((7,)),
            dma((3,)),
            dma((3,)),
        ],
        compiler_params=pltpu.CompilerParams(
            collective_id=level, has_side_effects=True, vmem_limit_bytes=52 * 2**20
        ),
    )(*args)


def on_device(cache_pool, fresh_kv, queries, stretch_owner, stretch_slot, recomp):
    pool, fresh, q = cache_pool[0, 0], fresh_kv[0], queries[0]
    small = [jnp.transpose(a.reshape(-1, 2)) for a in (stretch_owner, stretch_slot, recomp)]
    tab, level, *swapped = prepare_call(*small, pool, fresh, q)
    out, dev = lax.switch(
        level[0],
        [functools.partial(whole_call, i) for i in range(len(LEVELS))],
        tab, pool, fresh, q, *swapped,
    )
    return out[None], dev


def solution(mesh):
    placed = (
        P("seq", "req", "tp", None, None, None),
        P("req", "tp", "seq", None),
        P("req", "seq", "tp"),
        P(),
        P(),
        P(),
    )
    return jax.shard_map(
        on_device,
        mesh=mesh,
        in_specs=placed,
        out_specs=(P("req", "seq", "tp"), P("req", "seq")),
        check_vma=False,
    )
```

time: 90.3 us -> 91.8 us (1.017)
  Pallas kernels: 87.3 us -> 88.6 us
    pallas_call x1, Pallas kernels: 6.12 us -> 8.2 us  [prepare_call(): pl.pallas_call(prepare_kernel, out_shape=(jax.ShapeDtypeStruct((131,), wo...]
where the time goes in v1:
time: 91.8 us; the launch traced here: 91.6 us
  Pallas kernels  88.6 us (97%)
  local copies, waits for them, and re-layouts  1.4 us (2%)
  between operations  1.39 us (2%)
    pallas_call x1, Pallas kernels, whole_call(): pl.pallas_call(functools.partial(whole_kernel, caps), out_shape=(jax.Shap...  80.4 us
    pallas_call x1, Pallas kernels, prepare_call(): pl.pallas_call(prepare_kernel, out_shape=(jax.ShapeDtypeStruct((131,), wo...  8.2 us

profile of v1, /device:TPU:1, one launch (start us, length us, event | category | flops | bytes accessed | tf_op | source)
XLA Modules:
  0.0 91.6 jit_solution(12014985891186714785)
XLA Ops:
  0.6 0.0 copy-start.1
  0.6 0.0 copy-start.2
  0.7 0.0 copy-start
  0.7 8.2 %shard_map.77 = (s32[131]{0:T(256)S(1)}, s32[1]{0:T(128)}, bf16[16,128,256]{2,1,0:T(8,128)(2,1)}, bf16[128,256]{1,0:T(8,128)(2,1)S(1)}, bf16[128,1536]{1,0:T(8,128)(2,1)S(1)}) custom-call(s32[2,32]{1,0:T(2,128)} %bitcast.37, s32[2,32]{1,0:T(2,128)} %bitcast.38, s32[2,32]{1,0:T(2,128)} %bitcast.39, bf16[2,16,128,256]{3,2,1,0:T(8,128)(2,1)} %bitcast.14, ...), custom_call_target="tpu_custom_call" | custom-call | tf_op jit(solution)/shard_map/pallas_call | solution.py:173
  9.6 0.0 copy-done.1
  9.6 0.0 copy-done.2
  9.6 0.0 copy-done
  9.6 80.6 %conditional.1 = (f32[1,128]{1,0:T(1,128)S(1)}, bf16[1,128,3072]{2,1,0:T(8,128)(2,1)S(1)}) conditional(s32[]{:T(128)} %bitcast.12, (s32[131]{0:T(256)S(1)}, bf16[2,16,128,256]{3,2,1,0:T(8,128)(2,1)S(1)}, bf16[2,128,256]{2,1,0:T(8,128)(2,1)S(1)}, bf16[128,3072]{1,0:T(8,128)(2,1)S(1)}, bf16[16,128,256]{2,1,0:T(8,128)(2,1)}, ...), branch_computations={%region_0.0_spmd, %region_1.0_spmd, %region_2.0_spmd, %region_3.0_... | conditional | bytes 16 | solution.py:535
  9.6 80.4 %branch_2_fun.1 = (bf16[128,3072]{1,0:T(8,128)(2,1)S(1)}, f32[1,128]{1,0:T(1,128)S(1)}) custom-call(s32[131]{0:T(256)S(1)} %get-tuple-element.99.tab, bf16[2,16,128,256]{3,2,1,0:T(8,128)(2,1)S(1)} %get-tuple-element.100.pool, bf16[2,128,256]{2,1,0:T(8,128)(2,1)S(1)} %get-tuple-element.101.fresh, bf16[128,3072]{1,0:T(8,128)(2,1)S(1)} %get-tuple-element.102.q, ...), custom_call_target="tpu_custom_call" | custom-call | tf_op jit(solution)/shard_map/cond/branch_2_fun/pallas_call | solution.py:488
  90.2 0.9 copy.20
  91.1 0.5 copy.21
Async XLA Ops:
  0.6 8.9 %copy-start.1 = (bf16[1,128,3072]{2,1,0:T(8,128)(2,1)S(1)}, bf16[1,128,3072]{2,1,0:T(8,128)(2,1)}, u32[]{:S(2)}) copy-start(bf16[1,128,3072]{2,1,0:T(8,128)(2,1)} %param.13) | copy-start | bytes 2359300
  0.6 8.9 %copy-start.2 = (bf16[1,2,128,256]{3,2,1,0:T(8,128)(2,1)S(1)}, bf16[1,2,128,256]{3,2,1,0:T(8,128)(2,1)}, u32[]{:S(2)}) copy-start(bf16[1,2,128,256]{3,2,1,0:T(8,128)(2,1)} %param.12) | copy-start | bytes 393220
  0.7 8.9 %copy-start = (bf16[1,1,2,16,128,256]{5,4,3,2,1,0:T(8,128)(2,1)S(1)}, bf16[1,1,2,16,128,256]{5,4,3,2,1,0:T(8,128)(2,1)}, u32[]{:S(2)}) copy-start(bf16[1,1,2,16,128,256]{5,4,3,2,1,0:T(8,128)(2,1)} %param.11) | copy-start | bytes 6291460
